TPU v7x, 512 devices: a whole 4x8x8 slice. The times are simulated.
512 devices in a mesh: views: 4 (over x), depth: 32 (over y, z_hi), lat: 4 (over z_lo, core).
Axes of the slice: x: 4, y: 8, z: 8 (z_hi: 4, z_lo: 2; z = z_hi * 2 + z_lo), core: 2. Of those that a mesh axis runs over, the one named last changes fastest.
Arguments:
- density: bfloat16 [64, 2, 128, 2048], P(None, None, 'depth', 'lat'), may hold values from 0 to 3, as said below
- measured: float32 [16, 64, 2048], P('views', None, 'lat'), may hold values from 0 to 4
- shear_shift: int32 [16, 128], P('views', 'depth'), may hold values from -64 to 63
- shear_frac: float32 [16, 128], P('views', 'depth'), may hold values from 0 to 1
- spectrum: float32 [64], replicated, may hold values from 0.05 to 1
- attenuation: float32 [2, 64], replicated, may hold values from 0.3 to 6
Outputs:
- density_gradient: float32 [64, 2, 128, 2048], P('views', None, 'depth', 'lat')
Inputs may be any that keep to these rules, and one draw needn't show every extreme that they name: `density`: densities are non-negative.
All inputs are finite; a program needn't handle non-finite values.
Results may differ from a plain program's by a relative error of at most 0.0016.
Values may be sent and summed in bfloat16 or wider, within the bound.
A program may use at most 64 MiB of HBM per device.

v0:
```python
import jax
import jax.numpy as jnp
from jax import lax
from jax.sharding import PartitionSpec as P

HALO = 64


def with_halo(x, sides, width):
    for axis, dim in sides:
        size, length = (lax.axis_size(axis), x.shape[dim])
        up = [(i, (i + 1) % size) for i in range(size - 1)]
        down = [(j, i) for i, j in up]
        last = lax.slice_in_dim(x, length - width, length, axis=dim)
        first = lax.slice_in_dim(x, 0, width, axis=dim)
        before = lax.ppermute(last, axis, up)
        after = lax.ppermute(first, axis, down)
        x = jnp.concatenate([before, x, after], axis=dim)
    return x


def band_forward(shear_shift, lower_weight, upper_weight, window, block_width):
    band_shape = (shear_shift.shape[1], window, shear_shift.shape[0], block_width)
    tap_index = lax.broadcasted_iota(jnp.int32, band_shape, 1)
    column = lax.broadcasted_iota(jnp.int32, band_shape, 3)
    anchor = (shear_shift.T + HALO)[:, None, :, None]
    nothing = jnp.zeros((), jnp.bfloat16)
    lower_part = jnp.where(tap_index == column + anchor, lower_weight.T[:, None, :, None], nothing)
    upper_part = jnp.where(
        tap_index == column + anchor + 1, upper_weight.T[:, None, :, None], nothing
    )
    return lower_part + upper_part


def band_backward(shear_shift, lower_weight, upper_weight, window, block_width):
    band_shape = (shear_shift.shape[0], window, shear_shift.shape[1], block_width)
    tap_index = lax.broadcasted_iota(jnp.int32, band_shape, 1)
    column = lax.broadcasted_iota(jnp.int32, band_shape, 3)
    anchor = (HALO - shear_shift)[:, None, :, None]
    nothing = jnp.zeros((), jnp.bfloat16)
    lower_part = jnp.where(tap_index == column + anchor, lower_weight[:, None, :, None], nothing)
    upper_part = jnp.where(
        tap_index == column + anchor - 1, upper_weight[:, None, :, None], nothing
    )
    return lower_part + upper_part


def spectral(path_sums, observed, spectrum, attenuation, views_all):
    view_count, row_count, materials, tile_width = path_sums.shape
    block_pixels = 4096
    path_water = path_sums[:, :, 0, :].reshape(-1, block_pixels)
    path_bone = path_sums[:, :, 1, :].reshape(-1, block_pixels)
    target_flat = observed.reshape(-1, block_pixels)
    coefficients = jnp.concatenate(
        [jnp.ones((1, spectrum.shape[0]), jnp.float32), attenuation], axis=0
    )
    emitted = jnp.log(jnp.sum(spectrum))

    def one_block(inputs):
        water_block, bone_block, target_block = inputs
        exponent = (
            attenuation[0][:, None] * water_block[None, :]
            + attenuation[1][:, None] * bone_block[None, :]
        )
        counts = spectrum[:, None] * jnp.exp(-exponent)
        moments = jnp.dot(coefficients, counts, precision=lax.Precision.HIGHEST)
        intensity = moments[0]
        residual = emitted - jnp.log(intensity) - target_block
        factor = residual / intensity / views_all
        return (moments[1:] * factor[None, :]).astype(jnp.bfloat16)

    stacked = lax.map(one_block, (path_water, path_bone, target_flat))
    gradients = jnp.swapaxes(stacked, 0, 1).reshape(materials, view_count, row_count, tile_width)
    return jnp.transpose(gradients, (1, 2, 0, 3))


def per_device(density, measured, shear_shift, shear_frac, spectrum, attenuation):
    row_total, materials, depth_here, tile_width = density.shape
    block_width = min(128, tile_width)
    block_count = tile_width // block_width
    window = block_width + 2 * HALO
    views_all = measured.shape[0] * lax.axis_size("views")
    depth_all = depth_here * lax.axis_size("depth")
    rows_out = row_total // lax.axis_size("views")
    lower_weight = (1.0 - shear_frac).astype(jnp.bfloat16)
    upper_weight = shear_frac.astype(jnp.bfloat16)
    rows_here = density.shape[0]
    padded = with_halo(density, (("lat", 3),), HALO)
    framed = jnp.stack(
        [
            padded[:, :, :, number * block_width : number * block_width + window]
            for number in range(block_count)
        ],
        axis=2,
    )
    forward_band = band_forward(shear_shift, lower_weight, upper_weight, window, block_width)
    partial_value = jnp.einsum(
        "ymnzi,zivc->vymnc", framed, forward_band, preferred_element_type=jnp.float32
    )
    partial_value = partial_value.reshape(shear_shift.shape[0], rows_here, materials, tile_width)
    path_sums = lax.psum(partial_value, "depth") / depth_all
    path_grads = spectral(path_sums, measured, spectrum, attenuation, views_all)
    padded_grads = with_halo(path_grads, (("lat", 3),), HALO)
    framed_grads = jnp.stack(
        [
            padded_grads[:, :, :, number * block_width : number * block_width + window]
            for number in range(block_count)
        ],
        axis=3,
    )
    backward_band = band_backward(shear_shift, lower_weight, upper_weight, window, block_width)
    product = jnp.einsum(
        "vymni,vizc->ymznc", framed_grads, backward_band, preferred_element_type=jnp.float32
    )
    return lax.psum_scatter(
        product.reshape(rows_out * lax.axis_size("views"), materials, depth_here, tile_width),
        "views",
        scatter_dimension=0,
        tiled=True,
    )


def solution(mesh):
    in_specs = (
        P(None, None, "depth", "lat"),
        P("views", None, "lat"),
        P("views", "depth"),
        P("views", "depth"),
        P(),
        P(),
    )
    out_specs = P("views", None, "depth", "lat")
    return jax.shard_map(
        per_device, mesh=mesh, in_specs=in_specs, out_specs=out_specs, check_vma=False
    )
```

profile of v0, /device:TPU:8, one launch (start us, length us, event | category | flops | bytes accessed | tf_op | source)
XLA Modules:
  0.0 428.9 jit_solution(15175280310267215764)
XLA Ops:
  6.5 1.2 copy.23
  7.8 0.1 fusion.63
  7.9 1.7 collective-permute-start
  9.6 1.3 collective-permute-start.1
  11.0 4.0 collective-permute-done.1
  15.0 0.6 fusion.54
  15.6 1.1 convolution_bitcast_fusion.2
  16.7 1.1 copy.42
  18.0 1.0 copy-done
  18.9 0.1 reshape.22
  19.0 0.6 reduce_sum.9
  20.3 321.3 %all-reduce.3.cloned.1.call-done = f32[4,64,2,512]{3,1,2,0:T(8,128)} async-done(((f32[4,64,2,512]{3,1,2,0:T(8,128)}), f32[4,64,2,512]{3,1,2,0:T(8,128)}) %all-reduce.3.cloned.1.call-update) | async-done | bytes 1048592 | tf_op jit(solution)/shard_map/psum | solution.py:101
  341.6 1.4 broadcast_multiply_fusion
  343.0 0.1 fusion.61
  343.1 0.1 reshape_squeeze.6
  343.2 0.1 reshape_squeeze.7
  343.3 35.3 %while.10 = (s32[]{:T(128)}, bf16[32,2,4096]{2,1,0:T(2,128)(2,1)S(1)}, f32[64]{0:T(128)S(1)}, f32[2,64]{1,0:T(2,128)S(1)}, f32[32,4096]{1,0:T(8,128)S(1)}, /*ind...) while((s32[]{:T(128)}, ...), condition=%wide.region_3.4_spmd, body=%wide.region_2.3_spmd.sunk | while | flops 10780674 | bytes 264821 | solution.py:72
  343.3 0.9 convolution_bitcast_fusion.4
  344.4 0.9 convolution_bitcast_fusion.4
  345.5 0.9 convolution_bitcast_fusion.4
  346.7 0.9 convolution_bitcast_fusion.4
  347.8 0.9 convolution_bitcast_fusion.4
  348.9 0.9 convolution_bitcast_fusion.4
  350.0 0.9 convolution_bitcast_fusion.4
  351.1 0.9 convolution_bitcast_fusion.4
  352.2 0.9 convolution_bitcast_fusion.4
  353.3 0.9 convolution_bitcast_fusion.4
  354.4 0.9 convolution_bitcast_fusion.4
  355.5 0.9 convolution_bitcast_fusion.4
  356.6 0.9 convolution_bitcast_fusion.4
  357.7 0.9 convolution_bitcast_fusion.4
  358.8 0.9 convolution_bitcast_fusion.4
  359.9 0.9 convolution_bitcast_fusion.4
  361.0 0.9 convolution_bitcast_fusion.4
  362.1 0.9 convolution_bitcast_fusion.4
  363.2 0.9 convolution_bitcast_fusion.4
  364.3 0.9 convolution_bitcast_fusion.4
  365.4 0.9 convolution_bitcast_fusion.4
  366.5 0.9 convolution_bitcast_fusion.4
  367.6 0.9 convolution_bitcast_fusion.4
  368.7 0.9 convolution_bitcast_fusion.4
  369.8 0.9 convolution_bitcast_fusion.4
  370.9 0.9 convolution_bitcast_fusion.4
  372.0 0.9 convolution_bitcast_fusion.4
  373.1 0.9 convolution_bitcast_fusion.4
  374.2 0.9 convolution_bitcast_fusion.4
  375.3 0.9 convolution_bitcast_fusion.4
  376.4 0.9 convolution_bitcast_fusion.4
  377.5 0.9 convolution_bitcast_fusion.4
  378.6 0.3 copy.30
  378.9 0.2 reshape.23
  379.1 0.1 fusion.62
  379.2 1.3 collective-permute-start.2
  380.5 1.3 collective-permute-start.3
  381.8 0.1 copy.21
  381.9 0.1 copy.22
  382.1 0.1 copy.20
  382.1 3.1 collective-permute-done.3
  385.2 0.6 fusion.52
  385.8 1.1 convolution_bitcast_fusion.1
  386.9 0.7 copy.34
  387.6 1.4 reshape.24
  389.0 31.2 %reduce-scatter.2.cloned.1.call-done = f32[16,2,4,512]{3,0,2,1:T(8,128)} async-done(((f32[64,2,4,512]{3,0,2,1:T(8,128)}), f32[16,2,4,512]{3,0,2,1:T(8,128)}) %reduce-scatter.2.cloned.1.call-update) | async-done | bytes 262160 | tf_op jit(solution)/shard_map/reduce_scatter | solution.py:115
  420.3 1.8 copy.35
  (147 shorter events, 4.5 us)
Async XLA Ops:
  6.5 4.4 %copy-start.2 = (s32[4,4]{1,0:T(4,128)S(1)}, s32[4,4]{1,0:T(4,128)}, u32[]{:S(2)}) copy-start(s32[4,4]{1,0:T(4,128)} %param.10) | copy-start | bytes 196
  6.5 4.4 %copy-start.3 = (f32[4,4]{1,0:T(4,128)S(1)}, f32[4,4]{1,0:T(4,128)}, u32[]{:S(2)}) copy-start(f32[4,4]{1,0:T(4,128)} %param.11) | copy-start | bytes 196
  6.5 335.1 %all-reduce.3.cloned.1.call-start = ((), (), s32[]{:S(2)}) async-start(), calls=%async_computation.1 | async-start | bytes 2097152 | tf_op jit(solution)/shard_map/psum | solution.py:101
  7.9 3.1 collective-permute-start
  9.6 5.4 %collective-permute-start.1 = (bf16[64,2,4,64]{3,0,2,1:T(8,128)(2,1)S(1)}, bf16[64,2,4,64]{3,0,2,1:T(8,128)(2,1)S(1)}, u32[]{:S(2)}, u32[]{:S(2)}) collective-permute-start(bf16[64,2,4,64]{3,0,2,1:T(8,128)(2,1)S(1)} %get-tuple-element.88), channel_id=1, source_target_pairs={{1,0},{2,1},{3,2},{5,4},{6,5},{7,6},{9,8},{10,9},{11,10},{13,12},{... | collective-permute-start | bytes 196616 | tf_op jit(solution)/shard_map/ppermute | solution.py:17
  17.9 1.0 copy-start
  17.9 1.1 copy-start.4
  17.9 2.4 copy-start.1
  17.9 402.4 %reduce-scatter.2.cloned.1.call-start = ((), (), s32[]{:S(2)}) async-start(), calls=%async_computation.2 | async-start | bytes 1310720 | tf_op jit(solution)/shard_map/reduce_scatter | solution.py:115
  379.2 2.9 collective-permute-start.2
  380.5 4.7 %collective-permute-start.3 = (bf16[4,64,2,64]{3,1,0,2:T(8,128)(2,1)S(1)}, bf16[4,64,2,64]{3,1,0,2:T(8,128)(2,1)S(1)}, u32[]{:S(2)}, u32[]{:S(2)}) collective-permute-start(bf16[4,64,2,64]{3,1,0,2:T(8,128)(2,1)S(1)} %get-tuple-element.82), channel_id=1, source_target_pairs={{1,0},{2,1},{3,2},{5,4},{6,5},{7,6},{9,8},{10,9},{11,10},{13,12},{... | collective-permute-start | bytes 196616 | tf_op jit(solution)/shard_map/ppermute | solution.py:17
Sparse Core Ops, SparseCore 0:
  18.0 323.5 all-reduce.2
  389.1 31.0 reduce-scatter.1
where the time goes:
time: 429 us
  waiting for transfers between devices  360 us (84%)
  matrix products  31.8 us (7%)
  between operations  14.3 us (3%)
  local copies, waits for them, and re-layouts  9.82 us (2%)
  other arithmetic  6.36 us (1%)
  starting transfers between devices  5.67 us (1%)
    psum x1, waiting for transfers between devices, per_device(): path_sums = lax.psum(partial_value, 'depth') / depth_all  321 us
    reduce_scatter x1, waiting for transfers between devices, per_device(): lax.psum_scatter(product.reshape(rows_out * lax.axis_size('views'), mater...  31.2 us
    dot_general x32, matrix products, one_block(): moments = jnp.dot(coefficients, counts, precision=lax.Precision.HIGHEST)  29.5 us
  transfers between devices with their start and end apart: 6, of which 4 were waited for; matrix products, arithmetic and copies ran while one was open for 0% of the time, Pallas kernels for 0%

commit v1 on v0

--- a/solution.py
+++ b/solution.py
@@ -98,7 +98,7 @@
         "ymnzi,zivc->vymnc", framed, forward_band, preferred_element_type=jnp.float32
     )
     partial_value = partial_value.reshape(shear_shift.shape[0], rows_here, materials, tile_width)
-    path_sums = lax.psum(partial_value, "depth") / depth_all
+    path_sums = jnp.sum(lax.all_gather(partial_value, "depth"), axis=0) / depth_all
     path_grads = spectral(path_sums, measured, spectrum, attenuation, views_all)
     padded_grads = with_halo(path_grads, (("lat", 3),), HALO)
     framed_grads = jnp.stack(

time: 429 us -> 508 us (1.18)
  waiting for transfers between devices: 360 us -> 426 us
  other arithmetic: 6.36 us -> 18.8 us
    all_gather x0 -> x1, waiting for transfers between devices: none -> 391 us  [per_device(): lax.all_gather(partial_value, 'depth')]
    psum x1 -> x0, waiting for transfers between devices: 321 us -> none  [per_device(): path_sums = lax.psum(partial_value, 'depth') / depth_all]
    reduce_sum x0 -> x1, other arithmetic: none -> 12.3 us  [per_device(): jnp.sum(lax.all_gather(partial_value, 'depth'), axis=0) / depth_all]
where the time goes in v1:
time: 508 us
  waiting for transfers between devices  426 us (84%)
  matrix products  31.8 us (6%)
  other arithmetic  18.8 us (4%)
  between operations  14.3 us (3%)
  local copies, waits for them, and re-layouts  9.83 us (2%)
  starting transfers between devices  5.72 us (1%)
    all_gather x1, waiting for transfers between devices, per_device(): lax.all_gather(partial_value, 'depth')  391 us
    reduce_scatter x1, waiting for transfers between devices, per_device(): lax.psum_scatter(product.reshape(rows_out * lax.axis_size('views'), mater...  30.9 us
    dot_general x32, matrix products, one_block(): moments = jnp.dot(coefficients, counts, precision=lax.Precision.HIGHEST)  29.5 us
    reduce_sum x1, other arithmetic, per_device(): jnp.sum(lax.all_gather(partial_value, 'depth'), axis=0) / depth_all  12.3 us
  transfers between devices with their start and end apart: 6, of which 4 were waited for; matrix products, arithmetic and copies ran while one was open for 0% of the time, Pallas kernels for 0%

profile of v1, /device:TPU:8, one launch (start us, length us, event | category | flops | bytes accessed | tf_op | source)
XLA Modules:
  0.0 507.9 jit_solution(1377331811171550004)
XLA Ops:
  6.5 1.2 copy.39
  7.7 0.1 fusion.63
  7.8 1.7 collective-permute-start
  9.6 1.3 collective-permute-start.1
  10.9 0.7 broadcast_subtract_fusion
  11.6 0.8 subtract_convert_fusion
  12.4 2.6 collective-permute-done.1
  15.0 0.6 fusion.54
  15.6 1.1 convolution_bitcast_fusion.2
  16.7 0.7 copy.45
  17.4 1.4 all_gather_reshape.3
  18.9 0.1 reshape.18
  19.1 0.6 reduce_sum.19
  20.4 390.8 %all-gather.2.cloned.1.call-done = f32[32,4,64,2,512]{4,2,3,1,0:T(8,128)} async-done(((f32[1,4,64,2,512]{4,2,3,1,0:T(8,128)}), f32[32,4,64,2,512]{4,2,3,1,0:T(8,128)}) %all-gather.2.cloned.1.call-update) | async-done | bytes 33554448 | tf_op jit(solution)/shard_map/all_gather | solution.py:101
  411.2 12.3 %reduce_sum.18 = f32[4,64,2,512]{3,1,2,0:T(8,128)S(1)} reduce(f32[32,4,64,2,512]{4,2,3,1,0:T(8,128)} %all-gather.2.cloned.1.call-done, f32[]{:T(128)} %constant.31.clone.1), dimensions={0}, to_apply=%region_0.1 | reduce | flops 8126464 | bytes 34603012 | tf_op jit(solution)/shard_map/reduce_sum | solution.py:101
  423.5 0.1 broadcast_multiply_fusion
  423.6 0.1 fusion.61
  424.0 35.3 %while.10 = (s32[]{:T(128)}, bf16[32,2,4096]{2,1,0:T(2,128)(2,1)S(1)}, f32[64]{0:T(128)S(1)}, f32[2,64]{1,0:T(2,128)S(1)}, f32[32,4096]{1,0:T(8,128)S(1)}, /*ind...) while((s32[]{:T(128)}, ...), condition=%wide.region_3.4_spmd, body=%wide.region_2.3_spmd.sunk | while | flops 10780674 | bytes 264821 | solution.py:72
  424.0 0.9 convolution_bitcast_fusion.4
  425.1 0.9 convolution_bitcast_fusion.4
  426.2 0.9 convolution_bitcast_fusion.4
  427.3 0.9 convolution_bitcast_fusion.4
  428.4 0.9 convolution_bitcast_fusion.4
  429.5 0.9 convolution_bitcast_fusion.4
  430.6 0.9 convolution_bitcast_fusion.4
  431.7 0.9 convolution_bitcast_fusion.4
  432.8 0.9 convolution_bitcast_fusion.4
  433.9 0.9 convolution_bitcast_fusion.4
  435.0 0.9 convolution_bitcast_fusion.4
  436.1 0.9 convolution_bitcast_fusion.4
  437.2 0.9 convolution_bitcast_fusion.4
  438.3 0.9 convolution_bitcast_fusion.4
  439.5 0.9 convolution_bitcast_fusion.4
  440.6 0.9 convolution_bitcast_fusion.4
  441.7 0.9 convolution_bitcast_fusion.4
  442.8 0.9 convolution_bitcast_fusion.4
  443.9 0.9 convolution_bitcast_fusion.4
  445.0 0.9 convolution_bitcast_fusion.4
  446.1 0.9 convolution_bitcast_fusion.4
  447.2 0.9 convolution_bitcast_fusion.4
  448.3 0.9 convolution_bitcast_fusion.4
  449.4 0.9 convolution_bitcast_fusion.4
  450.5 0.9 convolution_bitcast_fusion.4
  451.6 0.9 convolution_bitcast_fusion.4
  452.7 0.9 convolution_bitcast_fusion.4
  453.8 0.9 convolution_bitcast_fusion.4
  454.9 0.9 convolution_bitcast_fusion.4
  456.0 0.9 convolution_bitcast_fusion.4
  457.1 0.9 convolution_bitcast_fusion.4
  458.2 0.9 convolution_bitcast_fusion.4
  459.2 0.3 copy.46
  459.5 0.2 reshape.19
  459.8 0.1 fusion.62
  459.9 1.3 collective-permute-start.2
  461.3 1.3 collective-permute-start.3
  462.6 0.1 copy.37
  462.7 0.1 copy.38
  462.9 1.6 collective-permute-done.3
  464.5 0.6 fusion.52
  465.1 1.1 convolution_bitcast_fusion.1
  466.2 0.7 copy.50
  466.9 1.4 reshape.20
  468.3 30.9 %reduce-scatter.2.cloned.1.call-done = f32[16,2,4,512]{3,0,2,1:T(8,128)} async-done(((f32[64,2,4,512]{3,0,2,1:T(8,128)}), f32[16,2,4,512]{3,0,2,1:T(8,128)}) %reduce-scatter.2.cloned.1.call-update) | async-done | bytes 262160 | tf_op jit(solution)/shard_map/reduce_scatter | solution.py:115
  499.2 1.8 copy.51
  (145 shorter events, 4.8 us)
Async XLA Ops:
  6.5 404.7 %all-gather.2.cloned.1.call-start = ((), (), s32[]{:S(2)}) async-start(), calls=%async_computation.1 | async-start | bytes 34603008 | tf_op jit(solution)/shard_map/all_gather | solution.py:101
  7.8 4.5 collective-permute-start
  9.6 5.4 %collective-permute-start.1 = (bf16[64,2,4,64]{3,0,2,1:T(8,128)(2,1)S(1)}, bf16[64,2,4,64]{3,0,2,1:T(8,128)(2,1)S(1)}, u32[]{:S(2)}, u32[]{:S(2)}) collective-permute-start(bf16[64,2,4,64]{3,0,2,1:T(8,128)(2,1)S(1)} %get-tuple-element.88), channel_id=1, source_target_pairs={{1,0},{2,1},{3,2},{5,4},{6,5},{7,6},{9,8},{10,9},{11,10},{13,12},{... | collective-permute-start | bytes 196616 | tf_op jit(solution)/shard_map/ppermute | solution.py:17
  17.4 1.5 copy-start
  17.4 1.6 copy-start.2
  17.4 2.9 copy-start.1
  18.9 480.3 %reduce-scatter.2.cloned.1.call-start = ((), (), s32[]{:S(2)}) async-start(), calls=%async_computation.2 | async-start | bytes 1310720 | tf_op jit(solution)/shard_map/reduce_scatter | solution.py:115
  459.9 3.0 collective-permute-start.2
  461.3 3.2 collective-permute-start.3
Sparse Core Ops, SparseCore 0:
  19.0 392.1 all-gather.1
  468.4 30.7 reduce-scatter.1
